TPU v7x, 256 devices: a whole 4x4x8 slice. The times are simulated.
256 devices in a mesh: blk: 32 (over z_hi, y, core), head: 8 (over x, z_lo).
Axes of the slice: x: 4, y: 4, z: 8 (z_hi: 4, z_lo: 2; z = z_hi * 2 + z_lo), core: 2. Of those that a mesh axis runs over, the one named last changes fastest.
Arguments:
- tokens: bfloat16 [64, 256, 5120], P('blk', 'head'), may hold values from -6 to 6
- span_pos: int32 [64], replicated, may hold values from 0 to 63, each once
- w_query: bfloat16 [5120, 8192], P('blk', 'head'), may hold values from -0.05660047 to 0.05660047
- key_projection: bfloat16 [5120, 1024], P('blk', 'head'), may hold values from -0.05660047 to 0.05660047
- value_projection: bfloat16 [5120, 1024], P('blk', 'head'), may hold values from -0.078125 to 0.078125
- query_gain: float32 [128], replicated, may hold values from 0.3 to 4
- key_gain: float32 [128], replicated, may hold values from 0.3 to 4
Outputs:
- partial_out: float32 [64, 64, 256, 128], P('head', 'blk')
- log_sum: float32 [64, 64, 256], P('head', 'blk')
Inputs may be any that keep to these rules, and one draw needn't show every extreme that they name: `span_pos`: each of 0 to 63 once.
All inputs are finite; a program needn't handle non-finite values.
Results may differ from a plain program's by a relative error of at most 0.008.
Values may be sent and summed in bfloat16 or wider, within the bound.
A program may use at most 128 MiB of HBM per device.

v0:
```python
import jax
import jax.numpy as jnp
from jax import lax
from jax.sharding import PartitionSpec as P

CYCLE_STEP_COUNT = 3


ROPE_BASE = 1000000.0
EPSILON = 1e-06
NEGATIVE = -1e30


def for_sending(shard):
    return jax.tree.map(lambda a: a.astype(jnp.bfloat16) if a.dtype == jnp.float32 else a, shard)


def shifted(block, axis, distance):
    devices = range(lax.axis_size(axis))
    route = [((i - distance) % len(devices), i) for i in devices]
    return lax.ppermute(block, axis, route)


def norm_rotate(value_rows, gain_vector, position):
    head_width = value_rows.shape[-1]
    half_width = head_width // 2
    mean_sq = jnp.mean(value_rows * value_rows, axis=-1, keepdims=True)
    normed = value_rows * lax.rsqrt(mean_sq + EPSILON) * gain_vector
    frequency = ROPE_BASE ** (-(jnp.arange(half_width, dtype=jnp.float32) * 2.0 / head_width))
    angles = position.astype(jnp.float32)[:, None] * frequency[None, :]
    cosine = jnp.cos(angles)[:, None, :]
    sine_part = jnp.sin(angles)[:, None, :]
    first_half = normed[..., :half_width]
    second = normed[..., half_width:]
    return jnp.concatenate(
        [first_half * cosine - second * sine_part, second * cosine + first_half * sine_part],
        axis=-1,
    )


def attend_block(state, query_rows, key_rows, value_rows, query_pos, key_pos, scale):
    peak_old, total_old, accum_old = state
    scores = (
        jnp.einsum("qhgd,khd->hgqk", query_rows, key_rows, preferred_element_type=jnp.float32)
        * scale
    )
    visible = key_pos[None, :] <= query_pos[:, None]
    scores = jnp.where(visible, scores, NEGATIVE)
    peak_block = jnp.max(scores, axis=-1)
    weights_exp = jnp.where(visible, jnp.exp(scores - peak_block[..., None]), 0.0)
    total_block = jnp.sum(weights_exp, axis=-1)
    accum_block = jnp.einsum(
        "hgqk,khd->hgqd",
        weights_exp.astype(jnp.bfloat16),
        value_rows,
        preferred_element_type=jnp.float32,
    )
    peak_new = jnp.maximum(peak_old, peak_block)
    factor_old = jnp.exp(peak_old - peak_new)
    factor_block = jnp.exp(peak_block - peak_new)
    total_new = total_old * factor_old + total_block * factor_block
    accum_new = accum_old * factor_old[..., None] + accum_block * factor_block[..., None]
    return (peak_new, total_new, accum_new)


def shards(tokens, span_pos, w_query, key_projection, value_projection, query_gain, key_gain):
    grouped = lax.all_gather(tokens, "head", axis=1, tiled=True)
    num_spans, span_len, model_width = grouped.shape
    row_count = num_spans * span_len
    flat_rows = grouped.reshape(row_count, model_width)
    head_width = query_gain.shape[0]
    query_heads = w_query.shape[1] // head_width
    kv_heads = key_projection.shape[1] // head_width
    group_count = query_heads // kv_heads
    cycle_index = lax.axis_index("blk")
    cycle_size = lax.axis_size("blk")
    row_index = jnp.arange(span_len, dtype=jnp.int32)

    def block_positions(offset):
        source = (cycle_index - offset) % cycle_size
        own_spans = lax.dynamic_slice_in_dim(span_pos, source * num_spans, num_spans, 0)
        return (own_spans[:, None] * span_len + row_index[None, :]).reshape(row_count)

    positions = block_positions(0)
    full_query, full_key, full_value = (
        lax.all_gather(w_query, "blk", axis=0, tiled=True),
        lax.all_gather(key_projection, "blk", axis=0, tiled=True),
        lax.all_gather(value_projection, "blk", axis=0, tiled=True),
    )
    query_raw = jnp.dot(flat_rows, full_query, preferred_element_type=jnp.float32)
    key_raw = jnp.dot(flat_rows, full_key, preferred_element_type=jnp.float32)
    value_raw = jnp.dot(flat_rows, full_value, preferred_element_type=jnp.float32)
    query_rows = norm_rotate(
        query_raw.reshape(row_count, query_heads, head_width), query_gain, positions
    ).astype(jnp.bfloat16)
    query_rows = query_rows.reshape(row_count, kv_heads, group_count, head_width)
    key_rows = norm_rotate(
        key_raw.reshape(row_count, kv_heads, head_width), key_gain, positions
    ).astype(jnp.bfloat16)
    value_rows = value_raw.astype(jnp.bfloat16).reshape(row_count, kv_heads, head_width)
    scale = head_width ** (-0.5)
    state = (
        jnp.full((kv_heads, group_count, row_count), NEGATIVE, jnp.float32),
        jnp.zeros((kv_heads, group_count, row_count), jnp.float32),
        jnp.zeros((kv_heads, group_count, row_count, head_width), jnp.float32),
    )
    current = (key_rows, value_rows)
    for cycle_step in range(CYCLE_STEP_COUNT + 1):
        if cycle_step < CYCLE_STEP_COUNT:
            arriving = jax.tree.map(
                lambda part, own: part.astype(own.dtype),
                shifted(for_sending(current), "blk", 1),
                current,
            )
        key_pos = block_positions(cycle_step)
        state = attend_block(state, query_rows, current[0], current[1], positions, key_pos, scale)
        if cycle_step < CYCLE_STEP_COUNT:
            current = arriving
    peak, total, accum = state
    partial_out = (accum / total[..., None]).reshape(query_heads, num_spans, span_len, head_width)
    log_sum = (peak + jnp.log(total)).reshape(query_heads, num_spans, span_len)
    return (partial_out, log_sum)


def solution(mesh):
    placed = (
        P("blk", "head", None),
        P(),
        P("blk", "head"),
        P("blk", "head"),
        P("blk", "head"),
        P(),
        P(),
    )
    return jax.shard_map(
        shards,
        mesh=mesh,
        in_specs=placed,
        out_specs=(P("head", "blk", None, None), P("head", "blk", None)),
        check_vma=False,
    )
```

profile of v0, /device:TPU:2, one launch (start us, length us, event | category | flops | bytes accessed | tf_op | source)
XLA Modules:
  0.0 413.9 jit_solution(1405187960772472466)
XLA Ops:
  7.2 0.0 all-gather.7.cloned.1.call-start
  7.2 0.7 all-gather.7.cloned.1.call-update
  7.9 0.0 all-gather.5.cloned.1.call-start
  8.0 0.7 all-gather.5.cloned.1.call-update
  8.7 0.0 all-gather.11.cloned.1.call-start
  8.7 0.7 all-gather.11.cloned.1.call-update
  9.4 0.0 all-gather.9.cloned.1.call-start
  9.4 0.5 all-gather.9.cloned.1.call-update
  10.0 0.9 dynamic-slice_multiply_fusion
  10.9 0.1 add_bitcast_fusion
  11.0 0.1 add_bitcast_fusion.2
  11.1 55.0 %all-gather.7.cloned.1.call-done = bf16[5120,128]{1,0:T(8,128)(2,1)} async-done(((bf16[160,128]{1,0:T(8,128)(2,1)}), bf16[5120,128]{1,0:T(8,128)(2,1)}) %all-gather.7.cloned.1.call-update) | async-done | bytes 1310736 | tf_op jit(solution)/shard_map/all_gather | solution.py:87
  66.1 111.3 %all-gather.5.cloned.1.call-done = bf16[2,256,5120]{2,1,0:T(8,128)(2,1)} async-done(((bf16[2,32,5120]{2,1,0:T(8,128)(2,1)}), bf16[2,256,5120]{2,1,0:T(8,128)(2,1)}) %all-gather.5.cloned.1.call-update) | async-done | bytes 5242896 | tf_op jit(solution)/shard_map/all_gather | solution.py:67
  177.5 4.7 %multiply_reduce_fusion.1 = (f32[512]{0:T(512)S(1)}, f32[512,128]{0,1:T(8,128)S(1)}) fusion(bf16[512,5120]{1,0:T(8,128)(2,1)} %bitcast.146, bf16[5120,128]{1,0:T(8,128)(2,1)} %all-gather.7.cloned.1.call-done), kind=kOutput, calls=%fused_computation.44 | convolution fusion | flops 671219200 | bytes 6817792 | tf_op jit(solution)/shard_map/dot_general | solution.py:91
  182.2 0.1 multiply_bitcast_fusion
  182.3 0.6 fusion.35
  182.9 0.1 collective-permute-start
  183.0 50.6 %all-gather.11.cloned.1.call-done = bf16[5120,128]{1,0:T(8,128)(2,1)} async-done(((bf16[160,128]{1,0:T(8,128)(2,1)}), bf16[5120,128]{1,0:T(8,128)(2,1)}) %all-gather.11.cloned.1.call-update) | async-done | bytes 1310736 | tf_op jit(solution)/shard_map/all_gather | solution.py:88
  233.6 4.4 %convolution_convert_fusion = bf16[512,128]{1,0:T(8,128)(2,1)S(1)} fusion(bf16[512,5120]{1,0:T(8,128)(2,1)} %bitcast.147, bf16[5120,128]{1,0:T(8,128)(2,1)} %all-gather.11.cloned.1.call-done), kind=kOutput, calls=%fused_computation.35 | convolution fusion | flops 671154176 | bytes 6684672 | tf_op jit(solution)/shard_map/dot_general | solution.py:92
  238.0 0.3 collective-permute-start.1
  238.3 0.7 broadcast_compare_fusion
  239.0 0.0 collective-permute-done
  239.0 0.2 collective-permute-start.2
  239.2 7.5 %collective-permute-done.1 = bf16[512,1,128]{2,0,1:T(8,128)(2,1)S(1)} collective-permute-done((bf16[512,1,128]{2,0,1:T(8,128)(2,1)S(1)}, bf16[512,1,128]{2,0,1:T(8,128)(2,1)S(1)}, u32[]{:S(2)}, u32[]{:S(2)}) %collective-permute-start.1) | collective-permute-done | bytes 131104 | tf_op jit(solution)/shard_map/ppermute | solution.py:21
  246.7 0.0 collective-permute-start.3
  246.7 0.5 multiply_cosine_fusion
  247.3 2.7 collective-permute-done.2
  250.0 12.0 %collective-permute-done.3 = bf16[512,1,128]{2,0,1:T(8,128)(2,1)S(1)} collective-permute-done((bf16[512,1,128]{2,0,1:T(8,128)(2,1)S(1)}, bf16[512,1,128]{2,0,1:T(8,128)(2,1)S(1)}, u32[]{:S(2)}, u32[]{:S(2)}) %collective-permute-start.3) | collective-permute-done | bytes 131104 | tf_op jit(solution)/shard_map/ppermute | solution.py:21
  262.1 0.0 collective-permute-start.5
  262.1 64.5 %all-gather.9.cloned.1.call-done = bf16[5120,1024]{1,0:T(8,128)(2,1)} async-done(((bf16[160,1024]{1,0:T(8,128)(2,1)}), bf16[5120,1024]{1,0:T(8,128)(2,1)}) %all-gather.9.cloned.1.call-update) | async-done | bytes 10485776 | tf_op jit(solution)/shard_map/all_gather | solution.py:86
  326.6 13.7 %copy.9 = bf16[1024,5120]{1,0:T(8,128)(2,1)} copy(bf16[1024,5120]{0,1:T(8,128)(2,1)} %bitcast.149) | data formatting | bytes 20971520 | tf_op jit(solution)/shard_map/dot_general | solution.py:90
  340.3 9.9 %multiply_reduce_fusion = (f32[512,8]{0,1:T(8,128)S(1)}, f32[512,8,128]{0,2,1:T(8,128)S(1)}) fusion(bf16[512,5120,1]{1,0,2:T(8,128)(2,1)} %bitcast.148, bf16[8,128,5120]{2,1,0:T(8,128)(2,1)} %bitcast.150), kind=kOutput, calls=%fused_computation.34 | convolution fusion | flops 5369753600 | bytes 17842176 | tf_op jit(solution)/shard_map/dot_general | solution.py:90
  350.3 0.5 multiply_multiply_fusion
  350.8 0.4 subtract_convert_fusion
  351.1 1.6 fusion
  352.7 2.0 fusion.4
  354.8 3.7 fusion.16
  358.5 4.8 %fusion.1 = (f32[8,512]{1,0:T(8,128)S(1)}, f32[512,512,8]{1,0,2:T(8,128)}) fusion(pred[512,512]{0,1:T(8,128)(4,1)S(1)} %get-tuple-element.21, bf16[512,8,64]{0,2,1:T(8,128)(2,1)S(1)} %get-tuple-element.10, bf16[512,8,64]{0,2,1:T(8,128)(2,1)S(1)} %get-tuple-element.9, bf16[512,1,128]{0,2,1:T(8,128)(2,1)S(1)} %collective-permute-done), kind=kOutput, calls=%fused_computation.9 | convolution fusion | flops 545255424 | bytes 9846784 | tf_op jit(solution)/shard_map/qhgd,khd->hgqk/dot_general | solution.py:44
  363.3 4.8 %fusion.3 = (f32[8,512]{1,0:T(8,128)S(1)}, f32[512,512,8]{1,0,2:T(8,128)}) fusion(pred[512,512]{0,1:T(8,128)(4,1)S(1)} %get-tuple-element.18, bf16[512,8,64]{0,2,1:T(8,128)(2,1)S(1)} %get-tuple-element.10, bf16[512,8,64]{0,2,1:T(8,128)(2,1)S(1)} %get-tuple-element.9, bf16[512,1,128]{0,2,1:T(8,128)(2,1)S(1)} %collective-permute-done.4), kind=kOutput, calls=%fused_computation.11 | convolution fusion | flops 545255424 | bytes 9846784 | tf_op jit(solution)/shard_map/qhgd,khd->hgqk/dot_general | solution.py:44
  368.1 4.7 %fusion.10 = f32[8,512]{1,0:T(8,128)S(1)} fusion(f32[512,512,8]{1,0,2:T(8,128)} %get-tuple-element.37, f32[8,512]{1,0:T(8,128)S(1)} %get-tuple-element.36, pred[512,512]{0,1:T(8,128)(4,1)S(1)} %get-tuple-element.18), kind=kLoop, calls=%fused_computation.18 | loop fusion | flops 10481664 | bytes 8683520 | tf_op jit(solution)/shard_map/reduce_sum | solution.py:51
  372.9 4.8 %fusion.2 = (f32[8,512]{1,0:T(8,128)S(1)}, f32[512,512,8]{1,0,2:T(8,128)}) fusion(pred[512,512]{0,1:T(8,128)(4,1)S(1)} %get-tuple-element.19, bf16[512,8,64]{0,2,1:T(8,128)(2,1)S(1)} %get-tuple-element.10, bf16[512,8,64]{0,2,1:T(8,128)(2,1)S(1)} %get-tuple-element.9, bf16[512,1,128]{0,2,1:T(8,128)(2,1)S(1)} %collective-permute-done.2), kind=kOutput, calls=%fused_computation.10 | convolution fusion | flops 545255424 | bytes 9846784 | tf_op jit(solution)/shard_map/qhgd,khd->hgqk/dot_general | solution.py:44
  377.7 4.5 %fusion.8 = f32[8,512]{1,0:T(8,128)S(1)} fusion(f32[512,512,8]{1,0,2:T(8,128)} %get-tuple-element.31, f32[8,512]{1,0:T(8,128)S(1)} %get-tuple-element.30, pred[512,512]{0,1:T(8,128)(4,1)S(1)} %get-tuple-element.19), kind=kLoop, calls=%fused_computation.16 | loop fusion | flops 10481664 | bytes 8683520 | tf_op jit(solution)/shard_map/reduce_sum | solution.py:51
  382.2 4.5 %fusion.6 = f32[8,512]{1,0:T(8,128)S(1)} fusion(f32[512,512,8]{1,0,2:T(8,128)} %get-tuple-element.33, f32[8,512]{1,0:T(8,128)S(1)} %get-tuple-element.32, pred[512,512]{0,1:T(8,128)(4,1)S(1)} %get-tuple-element.21), kind=kLoop, calls=%fused_computation.14 | loop fusion | flops 10481664 | bytes 8683520 | tf_op jit(solution)/shard_map/reduce_sum | solution.py:51
  386.8 5.9 %fusion.20 = f32[8,512,128]{2,1,0:T(8,128)S(1)} fusion(f32[512,512,8]{1,0,2:T(8,128)} %get-tuple-element.31, f32[8,512]{1,0:T(8,128)S(1)} %get-tuple-element.30, pred[512,512]{0,1:T(8,128)(4,1)S(1)} %get-tuple-element.19, bf16[512,1,128]{2,0,1:T(8,128)(2,1)S(1)} %collective-permute-done.3), kind=kOutput, calls=%fused_computation.26 | convolution fusion | flops 547356672 | bytes 10895360 | tf_op jit(solution)/shard_map/hgqk,khd->hgqd/dot_general | solution.py:52
  392.7 0.0 copy-start.2
  392.7 5.9 %fusion.18 = f32[8,512,128]{2,1,0:T(8,128)S(1)} fusion(f32[512,512,8]{1,0,2:T(8,128)} %get-tuple-element.33, f32[8,512]{1,0:T(8,128)S(1)} %get-tuple-element.32, pred[512,512]{0,1:T(8,128)(4,1)S(1)} %get-tuple-element.21, bf16[512,1,128]{2,0,1:T(8,128)(2,1)S(1)} %collective-permute-done.1), kind=kOutput, calls=%fused_computation.25 | convolution fusion | flops 547356672 | bytes 10895360 | tf_op jit(solution)/shard_map/hgqk,khd->hgqd/dot_general | solution.py:52
  398.6 0.7 log_add_fusion
  399.4 8.0 %add_divide_fusion = f32[8,512,128]{2,1,0:T(8,128)} fusion(f32[8,512,128]{2,1,0:T(8,128)S(1)} %fusion.20, f32[8,512,128]{2,1,0:T(8,128)S(1)} %fusion.18, f32[8,512,128]{2,1,0:T(8,128)S(1)} %copy-done.2, f32[512,512,8]{1,0,2:T(8,128)S(1)} %bitcast.152, f32[8,512]{1,0:T(8,128)S(1)} %get-tuple-element.36, pred[512,512]{0,1:T(8,128)(4,1)S(1)} %get-tuple-element.18, ...), kind=kOutput, calls=%fused_computation.32 | convolution fusion | flops 553648128 | bytes 17334272 | tf_op jit(solution)/shard_map/hgqk,khd->hgqd/dot_general | solution.py:52
  (32 shorter events, 0.3 us)
Async XLA Ops:
  7.2 175.1 %copy-start = (f32[128]{0:T(128)S(1)}, f32[128]{0:T(128)}, u32[]{:S(2)}) copy-start(f32[128]{0:T(128)} %param.13) | copy-start | bytes 1540
  7.2 59.0 %all-gather.7.cloned.1.call-start = ((), (), s32[]{:S(2)}) async-start(), calls=%async_computation.1 | async-start | bytes 1351680 | tf_op jit(solution)/shard_map/all_gather | solution.py:87
  7.9 169.6 %all-gather.5.cloned.1.call-start = ((), (), s32[]{:S(2)}) async-start(), calls=%async_computation | async-start | bytes 5898240 | tf_op jit(solution)/shard_map/all_gather | solution.py:67
  8.7 224.9 %all-gather.11.cloned.1.call-start = ((), (), s32[]{:S(2)}) async-start(), calls=%async_computation.3 | async-start | bytes 1351680 | tf_op jit(solution)/shard_map/all_gather | solution.py:88
  9.4 317.2 %all-gather.9.cloned.1.call-start = ((), (), s32[]{:S(2)}) async-start(), calls=%async_computation.2 | async-start | bytes 10813440 | tf_op jit(solution)/shard_map/all_gather | solution.py:86
  182.9 56.1 %collective-permute-start = (bf16[512,1,128]{0,2,1:T(8,128)(2,1)S(1)}, bf16[512,1,128]{0,2,1:T(8,128)(2,1)S(1)}, u32[]{:S(2)}, u32[]{:S(2)}) collective-permute-start(bf16[512,1,128]{0,2,1:T(8,128)(2,1)S(1)} %pad_maximum_fusion.1), channel_id=1, source_target_pairs={{248,0},{0,8},{8,16},{16,24},{24,32},{32,40},{40,48},{48,56},{56,6... | collective-permute-start | bytes 393224 | tf_op jit(solution)/shard_map/ppermute | solution.py:21
  238.0 8.8 %collective-permute-start.1 = (bf16[512,1,128]{2,0,1:T(8,128)(2,1)S(1)}, bf16[512,1,128]{2,0,1:T(8,128)(2,1)S(1)}, u32[]{:S(2)}, u32[]{:S(2)}) collective-permute-start(bf16[512,1,128]{2,0,1:T(8,128)(2,1)S(1)} %bitcast.160), channel_id=1, source_target_pairs={{248,0},{0,8},{8,16},{16,24},{24,32},{32,40},{40,48},{48,56},{56,6... | collective-permute-start | bytes 393224 | tf_op jit(solution)/shard_map/ppermute | solution.py:21
  239.0 11.0 %collective-permute-start.2 = (bf16[512,1,128]{0,2,1:T(8,128)(2,1)S(1)}, bf16[512,1,128]{0,2,1:T(8,128)(2,1)S(1)}, u32[]{:S(2)}, u32[]{:S(2)}) collective-permute-start(bf16[512,1,128]{0,2,1:T(8,128)(2,1)S(1)} %collective-permute-done), channel_id=1, source_target_pairs={{248,0},{0,8},{8,16},{16,24},{24,32},{32,40},{40,48},{48,56},{56,6... | collective-permute-start | bytes 393224 | tf_op jit(solution)/shard_map/ppermute | solution.py:21
  246.7 15.3 %collective-permute-start.3 = (bf16[512,1,128]{2,0,1:T(8,128)(2,1)S(1)}, bf16[512,1,128]{2,0,1:T(8,128)(2,1)S(1)}, u32[]{:S(2)}, u32[]{:S(2)}) collective-permute-start(bf16[512,1,128]{2,0,1:T(8,128)(2,1)S(1)} %collective-permute-done.1), channel_id=1, source_target_pairs={{248,0},{0,8},{8,16},{16,24},{24,32},{32,40},{40,48},{48,56},{56,6... | collective-permute-start | bytes 393224 | tf_op jit(solution)/shard_map/ppermute | solution.py:21
  250.0 113.3 %collective-permute-start.4 = (bf16[512,1,128]{0,2,1:T(8,128)(2,1)S(1)}, bf16[512,1,128]{0,2,1:T(8,128)(2,1)S(1)}, u32[]{:S(2)}, u32[]{:S(2)}) collective-permute-start(bf16[512,1,128]{0,2,1:T(8,128)(2,1)S(1)} %collective-permute-done.2), channel_id=1, source_target_pairs={{248,0},{0,8},{8,16},{16,24},{24,32},{32,40},{40,48},{48,56},{56,6... | collective-permute-start | bytes 393224 | tf_op jit(solution)/shard_map/ppermute | solution.py:21
  262.1 137.3 %collective-permute-start.5 = (bf16[512,1,128]{2,0,1:T(8,128)(2,1)S(1)}, bf16[512,1,128]{2,0,1:T(8,128)(2,1)S(1)}, u32[]{:S(2)}, u32[]{:S(2)}) collective-permute-start(bf16[512,1,128]{2,0,1:T(8,128)(2,1)S(1)} %collective-permute-done.3), channel_id=1, source_target_pairs={{248,0},{0,8},{8,16},{16,24},{24,32},{32,40},{40,48},{48,56},{56,6... | collective-permute-start | bytes 393224 | tf_op jit(solution)/shard_map/ppermute | solution.py:21
  340.3 10.0 %copy-start.1 = (f32[128]{0:T(128)S(1)}, f32[128]{0:T(128)}, u32[]{:S(2)}) copy-start(f32[128]{0:T(128)} %param.12) | copy-start | bytes 1540
  386.8 12.6 %slice-start = ((s8[8388608]{0:T(1024)(128)(4,1)}), s8[4194304]{0:T(1024)(128)(4,1)S(1)}, s32[]{:S(2)}) async-start(s8[8388608]{0:T(1024)(128)(4,1)} %bitcast.151), calls=%async_computation.4 | async-start | bytes 8388608
  392.7 6.7 %slice-start.1 = ((s8[8388608]{0:T(1024)(128)(4,1)}), s8[4194304]{0:T(1024)(128)(4,1)S(1)}, s32[]{:S(2)}) async-start(s8[8388608]{0:T(1024)(128)(4,1)} %bitcast.151), calls=%async_computation.5 | async-start | bytes 8388608
  392.7 6.6 %copy-start.2 = (f32[8,512,128]{2,1,0:T(8,128)S(1)}, f32[8,512,128]{2,1,0:T(8,128)}, u32[]{:S(2)}) copy-start(f32[8,512,128]{2,1,0:T(8,128)} %fusion.16) | copy-start | bytes 6291460
Sparse Core Ops, SparseCore 0:
  10.6 55.5 all-gather.6
  67.9 109.4 all-gather.4
  180.0 53.5 all-gather.10
  236.0 90.6 all-gather.8
where the time goes:
time: 416 us; the launch traced here: 414 us
  waiting for transfers between devices  306 us (74%)
  matrix products  58.5 us (14%)
  other arithmetic  20.3 us (5%)
  between operations  14.1 us (3%)
  local copies, waits for them, and re-layouts  13.9 us (3%)
    all_gather x1, waiting for transfers between devices, shards(): grouped = lax.all_gather(tokens, 'head', axis=1, tiled=True)  111 us
    all_gather x1, waiting for transfers between devices, shards(): lax.all_gather(w_query, 'blk', axis=0, tiled=True)  64.5 us
    all_gather x1, waiting for transfers between devices, shards(): lax.all_gather(key_projection, 'blk', axis=0, tiled=True)  55 us
    all_gather x1, waiting for transfers between devices, shards(): lax.all_gather(value_projection, 'blk', axis=0, tiled=True)  50.6 us
    dot_general x4, matrix products, attend_block(): jnp.einsum('hgqk,khd->hgqd', weights_exp.astype(jnp.bfloat16), value_rows...  23.5 us
    ppermute x6, waiting for transfers between devices, shifted(): return lax.ppermute(block, axis, route)  22.3 us
    dot_general x4, matrix products, attend_block(): jnp.einsum('qhgd,khd->hgqk', query_rows, key_rows, preferred_element_type...  16 us
    reduce_sum x4, other arithmetic, attend_block(): total_block = jnp.sum(weights_exp, axis=-1)  15.7 us
  transfers between devices with their start and end apart: 10, of which 7 were waited for; matrix products, arithmetic and copies ran while one was open for 20% of the time, Pallas kernels for 0%

commit v1 on v0

v1 whole, which is shorter than its diff:
```python
import math

import jax
import jax.numpy as jnp
import numpy as np
from jax import lax
from jax.experimental import pallas as pl
from jax.experimental.pallas import tpu as pltpu
from jax.sharding import PartitionSpec as P

MESH = pl.DeviceIdType.MESH
ROPE_BASE = 1000000.0
EPSILON = 1e-06
MASKED = 1e30
BF16 = jnp.bfloat16
F32 = jnp.float32

MODEL = 5120
HEAD = 128
HEADS = 8
BLOCK = 256
SPANS = 64
ROWS = 160
HALF = 80
PART = 256
PARTS = 5
DEPTH = 8 * ROWS


def rope_tables():
    frequency = ROPE_BASE ** (-(np.arange(HEAD // 2, dtype=np.float64) * 2.0 / HEAD))
    frequency = np.concatenate([frequency, frequency])

    def table(positions):
        angles = positions[:, None].astype(np.float64) * frequency[None, :]
        return np.stack([np.cos(angles), np.sin(angles)]).astype(np.float32)

    return table(np.arange(SPANS) * BLOCK), table(np.arange(BLOCK))


def kernel(
    span_pos, tokens, w_query, w_key, w_value, gains, span_table, row_table,
    out, log_sum,
    X, W, kv, q, cosine, sine, scores, staged,
    local_sem, send_sem, recv_sem, out_sem,
):
    blk, head = lax.axis_index("blk"), lax.axis_index("head")
    z, y, c = blk // 8, (blk // 2) % 4, blk % 2
    x, l = head // 2, head % 2
    chip = blk // 2

    def place(z=z, y=y, c=c, x=x, l=l):
        return (z * 8 + y * 2 + c, x * 2 + l)

    zp, zm = place(z=(z + 1) % 4), place(z=(z + 3) % 4)
    yp, ym = place(y=(y + 1) % 4), place(y=(y + 3) % 4)
    xp, xm = place(x=(x + 1) % 4), place(x=(x + 3) % 4)
    lp, sib = place(l=1 - l), place(c=1 - c)
    nxt = (((chip + 1) % 16) * 2 + c, head)
    prv = (((chip + 15) % 16) * 2 + c, head)
    after = (((chip + 2) % 16) * 2, head)
    before = (((chip + 14) % 16) * 2 + 1, head)
    third = jnp.where(c == 0, sib[0], after[0])

    own = [pltpu.make_async_copy(w_key, W.at[0, 0, y, c, :, pl.ds(0, HEAD)], local_sem.at[0]),
           pltpu.make_async_copy(w_value, W.at[0, 0, y, c, :, pl.ds(HEAD, HEAD)], local_sem.at[1])]
    for p in range(1, PARTS):
        own.append(pltpu.make_async_copy(
            w_query.at[:, pl.ds((p - 1) * PART, PART)], W.at[p, 0, y, c], local_sem.at[1 + p]))
    own.append(pltpu.make_async_copy(tokens, X.at[:, x, l], local_sem.at[PARTS + 1]))
    for copy in own:
        copy.start()

    barrier = pltpu.get_barrier_semaphore()
    for device in (zp, zm, yp, ym, xp, xm, lp, sib, prv):
        pl.semaphore_signal(barrier, inc=1, device_id=device, device_id_type=MESH)

    @pl.when(c == 0)
    def _():
        pl.semaphore_signal(barrier, inc=1, device_id=before, device_id_type=MESH)

    pl.semaphore_wait(barrier, 9 + c)
    for copy in own:
        copy.wait()

    started = []

    def send(src, dst, device):
        n = len(started)
        copy = pltpu.make_async_remote_copy(
            src_ref=src, dst_ref=dst, send_sem=send_sem.at[n], recv_sem=recv_sem.at[n],
            device_id=device, device_id_type=MESH)
        copy.start()
        started.append(copy)
        return copy

    A, B = pl.ds(0, HALF), pl.ds(HALF, HALF)
    y_below, y_above = (y + 3) % 4, (y + 1) % 4
    x_below, x_above = (x + 3) % 4, (x + 1) % 4

    def z_send(p, places):
        return (send(W.at[p, 0, places, c], W.at[p, 1, places, c], zp),
                send(W.at[p, 0, places, c], W.at[p, 2, places, c], zm))

    def z_forward(p, places, copies):
        copies[0].wait_recv()
        first = send(W.at[p, 1, places, c, A], W.at[p, 3, places, c, A], zp)
        copies[1].wait_recv()
        return (first, send(W.at[p, 2, places, c, B], W.at[p, 3, places, c, B], zm))

    def y_send(p, slots):
        return (send(W.at[p, slots, y, c], W.at[p, slots, y, c], yp),
                send(W.at[p, slots, y, c], W.at[p, slots, y, c], ym))

    def y_forward(p, slots, copies):
        copies[0].wait_recv()
        first = send(W.at[p, slots, y_below, c, A], W.at[p, slots, y_below, c, A], yp)
        copies[1].wait_recv()
        return (first, send(W.at[p, slots, y_above, c, B], W.at[p, slots, y_above, c, B], ym))

    def x_send(lane):
        return (send(X.at[0, x, lane], X.at[0, x, lane], xp),
                send(X.at[1, x, lane], X.at[1, x, lane], xm),
                send(X.at[1, x, lane], X.at[1, x, lane], xp),
                send(X.at[0, x, lane], X.at[0, x, lane], xm))

    def x_forward(lane, copies):
        copies[0].wait_recv()
        first = send(X.at[0, x_below, lane], X.at[0, x_below, lane], xp)
        copies[1].wait_recv()
        return (first, send(X.at[1, x_above, lane], X.at[1, x_above, lane], xm))

    def core_send(p):
        return send(W.at[p, :, :, c], W.at[p, :, :, c], sib)

    def arrive(*copies):
        for copy in copies:
            copy.wait_recv()

    first_slot, other_slots, all_slots = pl.ds(0, 1), pl.ds(1, 3), pl.ds(0, 4)
    every_y = pl.ds(0, 4)

    def tables():
        for s in range(2):
            chosen = lax.broadcasted_iota(jnp.int32, (SPANS, HEAD), 0) == span_pos[blk * 2 + s]
            span_cos = jnp.sum(jnp.where(chosen, span_table[0], 0.0), axis=0, keepdims=True)
            span_sin = jnp.sum(jnp.where(chosen, span_table[1], 0.0), axis=0, keepdims=True)
            cosine[s] = (span_cos * row_table[0] - span_sin * row_table[1]).reshape(4, 2, 32, HEAD)
            whole = span_sin * row_table[0] + span_cos * row_table[1]
            lane = lax.broadcasted_iota(jnp.int32, (BLOCK, HEAD), 1)
            sine[s] = jnp.where(lane < HEAD // 2, -whole, whole).reshape(4, 2, 32, HEAD)

    def project(p, lane):
        total = None
        for slot, place_z in enumerate((z, (z + 3) % 4, (z + 1) % 4, (z + 2) % 4)):
            depth = pl.ds(pl.multiple_of(place_z * DEPTH, DEPTH), DEPTH)
            rows = X[:, :, pl.ds(lane, 1), :, depth].reshape(BLOCK, DEPTH)
            term = jnp.dot(rows, W[p, slot].reshape(DEPTH, PART), preferred_element_type=F32)
            total = term if total is None else total + term
        return total

    def norm_rotate(raw, gain, lane):
        mean_sq = jnp.mean(raw * raw, axis=-1, keepdims=True)
        normed = raw * lax.rsqrt(mean_sq + EPSILON) * gain
        cos_rows = cosine[:, :, pl.ds(lane, 1)].reshape(BLOCK, HEAD)
        sin_rows = sine[:, :, pl.ds(lane, 1)].reshape(BLOCK, HEAD)
        turned = normed * cos_rows + pltpu.roll(normed, HEAD // 2, 1) * sin_rows
        return turned.astype(BF16).reshape(2, 4, 1, 32, HEAD)

    def keys_values(lane):
        raw = project(0, lane)
        kv[0, :, :, pl.ds(lane, 1), :, pl.ds(0, HEAD)] = norm_rotate(raw[:, :HEAD], gains[1:2], lane)
        kv[0, :, :, pl.ds(lane, 1), :, pl.ds(HEAD, HEAD)] = (
            raw[:, HEAD:].astype(BF16).reshape(2, 4, 1, 32, HEAD))

    def queries(p, lane):
        raw = project(p, lane)
        for j in range(2):
            q[2 * (p - 1) + j, :, :, pl.ds(lane, 1)] = norm_rotate(
                raw[:, j * HEAD:(j + 1) * HEAD], gains[0:1], lane)

    def kv_send(lane):
        ahead = send(kv.at[0, :, :, lane], kv.at[2, :, :, lane], nxt)
        slot = jnp.where(c == 0, 1, 3)
        return ahead, send(kv.at[0, :, :, lane], kv.at[slot, :, :, lane], (third, head))

    def kv_forward(lane, ahead):
        arrive(ahead)
        slot = jnp.where(c == 0, 3, 1)
        return send(kv.at[2, :, :, lane], kv.at[slot, :, :, lane], sib)

    z0 = z_send(0, y)
    y4 = y_send(4, first_slot)
    y0 = y_send(0, first_slot)
    x_own = x_send(l)
    x_lane = send(X.at[:, x, l], X.at[:, x, l], lp)
    z1 = z_send(1, y)
    tables()
    z0f = z_forward(0, y, z0)
    y4f = y_forward(4, first_slot, y4)
    y0f = y_forward(0, first_slot, y0)
    arrive(*z0f)
    y0r = y_send(0, other_slots)
    z1f = z_forward(1, y, z1)
    z2 = z_send(2, y)
    x_ownf = x_forward(l, x_own)
    arrive(x_lane)
    x_oth = x_send(1 - l)
    arrive(*z1f)
    y1 = y_send(1, all_slots)
    y0rf = y_forward(0, other_slots, y0r)
    z2f = z_forward(2, y, z2)
    z3 = z_send(3, y)
    arrive(*y0f, *y0rf)
    c0 = core_send(0)
    arrive(*z2f)
    y2 = y_send(2, all_slots)
    arrive(x_own[2], x_own[3], *x_ownf)
    arrive(c0)
    keys_values(l)
    kv_a, kv_a3 = kv_send(l)
    y1f = y_forward(1, all_slots, y1)
    z3f = z_forward(3, y, z3)
    arrive(*y4f)
    z4 = z_send(4, every_y)
    arrive(*z3f)
    y3 = y_send(3, all_slots)
    x_othf = x_forward(1 - l, x_oth)
    arrive(*y1f)
    c1 = core_send(1)
    kv_af = kv_forward(l, kv_a)
    y2f = y_forward(2, all_slots, y2)
    arrive(c1)
    queries(1, l)
    z4f = z_forward(4, every_y, z4)
    arrive(*y2f)
    c2 = core_send(2)
    arrive(x_oth[2], x_oth[3], *x_othf)
    keys_values(1 - l)
    kv_b, kv_b3 = kv_send(1 - l)
    y3f = y_forward(3, all_slots, y3)
    queries(1, 1 - l)
    arrive(c2)
    queries(2, l)
    kv_bf = kv_forward(1 - l, kv_b)
    queries(2, 1 - l)
    arrive(*z4f)
    c4 = core_send(4)
    arrive(*y3f)
    c3 = core_send(3)
    arrive(c4)
    queries(4, l)
    queries(4, 1 - l)
    arrive(c3)
    queries(3, l)
    queries(3, 1 - l)
    arrive(kv_a3, kv_af, kv_b3, kv_bf)

    own_pos = [span_pos[blk * 2 + s] for s in range(2)]
    offsets = []
    for step in range(4):
        source = (blk + 32 - step) % 32
        for s in range(2):
            pos = span_pos[source * 2 + s]
            offsets.append([jnp.where(pos <= own_pos[i], 0.0, MASKED).astype(F32) for i in range(2)])
    factor = HEAD ** (-0.5) * math.log2(math.e)
    causal = (lax.broadcasted_iota(jnp.int32, (BLOCK, BLOCK), 0)
              >= lax.broadcasted_iota(jnp.int32, (BLOCK, BLOCK), 1))

    def attend(h, carry):
        rows = q[h].reshape(2 * BLOCK, HEAD)
        peaks = [None, None]
        for tile in range(8):
            keys = kv[tile // 2, tile % 2, :, :, :, pl.ds(0, HEAD)].reshape(BLOCK, HEAD)
            found = lax.dot_general(rows, keys, (((1,), (1,)), ((), ())), preferred_element_type=F32) * factor
            for i in range(2):
                part = found[i * BLOCK:(i + 1) * BLOCK]
                if tile == i:
                    part = jnp.where(causal, part, -MASKED)
                scores[i, :, pl.ds(tile * BLOCK, BLOCK)] = part
                peak = jnp.maximum(part[:, :HEAD], part[:, HEAD:]) - offsets[tile][i]
                peaks[i] = peak if peaks[i] is None else jnp.maximum(peaks[i], peak)
        for i in range(2):
            peak = jnp.max(peaks[i], axis=-1, keepdims=True)
            total = jnp.zeros((BLOCK, HEAD), F32)
            summed = jnp.zeros((BLOCK, HEAD), F32)
            for tile in range(8):
                weights = jnp.exp2(scores[i, :, pl.ds(tile * BLOCK, BLOCK)] - (peak + offsets[tile][i]))
                total = total + (weights[:, :HEAD] + weights[:, HEAD:])
                values = kv[tile // 2, tile % 2, :, :, :, pl.ds(HEAD, HEAD)].reshape(BLOCK, HEAD)
                summed = summed + jnp.dot(weights.astype(BF16), values, preferred_element_type=F32)
            whole = jnp.sum(total, axis=-1, keepdims=True)
            staged[h, i] = summed / whole
            lse = peak * math.log(2.0) + jnp.log(whole)
            log_sum[h, pl.ds(i, 1), :] = jnp.transpose(jnp.broadcast_to(lse, (BLOCK, HEAD)))[0:1, :]
        pltpu.make_async_copy(staged.at[h], out.at[h], out_sem.at[h]).start()
        return carry

    lax.fori_loop(0, HEADS, attend, 0)

    def finish(h, carry):
        pltpu.make_async_copy(staged.at[h], out.at[h], out_sem.at[h]).wait()
        return carry

    lax.fori_loop(0, HEADS, finish, 0)
    for copy in started:
        copy.wait_send()


SENDS = 68


def shards(tokens, span_pos, w_query, key_projection, value_projection, query_gain, key_gain):
    span_table, row_table = rope_tables()
    gains = jnp.stack([query_gain, key_gain])
    vmem, anywhere = pl.BlockSpec(memory_space=pltpu.VMEM), pl.BlockSpec(memory_space=pl.ANY)
    return pl.pallas_call(
        kernel,
        out_shape=(
            jax.ShapeDtypeStruct((HEADS, 2, BLOCK, HEAD), F32),
            jax.ShapeDtypeStruct((HEADS, 2, BLOCK), F32),
        ),
        in_specs=[pl.BlockSpec(memory_space=pltpu.SMEM), anywhere, anywhere, anywhere, anywhere, vmem, vmem, vmem],
        out_specs=(anywhere, vmem),
        scratch_shapes=[
            pltpu.VMEM((2, 4, 2, 32, MODEL), BF16),
            pltpu.VMEM((PARTS, 4, 4, 2, ROWS, PART), BF16),
            pltpu.VMEM((4, 2, 4, 2, 32, 2 * HEAD), BF16),
            pltpu.VMEM((HEADS, 2, 4, 2, 32, HEAD), BF16),
            pltpu.VMEM((2, 4, 2, 32, HEAD), F32),
            pltpu.VMEM((2, 4, 2, 32, HEAD), F32),
            pltpu.VMEM((2, BLOCK, 8 * BLOCK), F32),
            pltpu.VMEM((HEADS, 2, BLOCK, HEAD), F32),
            pltpu.SemaphoreType.DMA((PARTS + 2,)),
            pltpu.SemaphoreType.DMA((SENDS,)),
            pltpu.SemaphoreType.DMA((SENDS,)),
            pltpu.SemaphoreType.DMA((HEADS,)),
        ],
        compiler_params=pltpu.CompilerParams(
            collective_id=0, has_side_effects=True, vmem_limit_bytes=56 * 2**20),
        name="layer",
    )(span_pos, tokens, w_query, key_projection, value_projection, gains, span_table, row_table)


def solution(mesh):
    placed = (
        P("blk", "head", None),
        P(),
        P("blk", "head"),
        P("blk", "head"),
        P("blk", "head"),
        P(),
        P(),
    )
    return jax.shard_map(
        shards,
        mesh=mesh,
        in_specs=placed,
        out_specs=(P("head", "blk", None, None), P("head", "blk", None)),
        check_vma=False,
    )
```

time: 416 us -> 129 us (0.31)
  waiting for transfers between devices: 306 us -> 0 us
  Pallas kernels: 0 us -> 123 us
  matrix products: 58.5 us -> 0 us
  other arithmetic: 20.3 us -> 1.24 us
  between operations: 14.1 us -> 0.65 us
  local copies, waits for them, and re-layouts: 13.9 us -> 3.73 us
    all_gather x4 -> x0, waiting for transfers between devices: 281 us -> none  [the longest x1 111 us: shards(): grouped = lax.all_gather(tokens, 'head', axis=1, tiled=True)]
    pallas_call x0 -> x1, Pallas kernels: none -> 123 us  [shards(): pl.pallas_call(kernel, out_shape=(jax.ShapeDtypeStruct((HEADS, 2, BLOCK,...]
    dot_general x11 -> x0, matrix products: 58.5 us -> none  [the longest x4 23.5 us: attend_block(): jnp.einsum('hgqk,khd->hgqd', weights_exp.astype(jnp.bfloat16), value_rows...]
    ppermute x6 -> x0, waiting for transfers between devices: 22.3 us -> none  [shifted(): return lax.ppermute(block, axis, route)]
    reduce_sum x4 -> x0, other arithmetic: 15.7 us -> none  [attend_block(): total_block = jnp.sum(weights_exp, axis=-1)]
    dot_general x1 -> x0, local copies, waits for them, and re-layouts: 13.7 us -> none  [shards(): jnp.dot(flat_rows, full_query, preferred_element_type=jnp.float32)]
  transfers between devices with their start and end apart: 10 -> 0, of which waited for: 7 -> 0; matrix products, arithmetic and copies ran while one was open for 20% -> 0% of each run, Pallas kernels for 0% -> 0%
where the time goes in v1:
time: 129 us
  Pallas kernels  123 us (95%)
  local copies, waits for them, and re-layouts  3.73 us (3%)
    pallas_call x1, Pallas kernels, shards(): pl.pallas_call(kernel, out_shape=(jax.ShapeDtypeStruct((HEADS, 2, BLOCK,...  123 us
    unnamed x4, local copies, waits for them, and re-layouts  3.73 us

profile of v1, /device:TPU:2, one launch (start us, length us, event | category | flops | bytes accessed | tf_op | source)
XLA Modules:
  0.0 128.8 jit_solution(12560244377420384225)
XLA Ops:
  0.6 1.2 pad_maximum_fusion.gains
  1.9 123.2 %layer.1 = (f32[8,2,256,128]{3,2,1,0:T(8,128)}, f32[8,2,256]{2,1,0:T(2,128)}) custom-call(s32[64]{0:T(128)} %span_pos.1, bf16[2,32,5120]{2,1,0:T(8,128)(2,1)} %tokens.1, bf16[160,1024]{1,0:T(8,128)(2,1)} %w_query.1, bf16[160,128]{1,0:T(8,128)(2,1)} %w_key.1, bf16[160,128]{1,0:T(8,128)(2,1)} %w_value.1, f32[2,128]{1,0:T(2,128)} %pad_maximum_fusion.gains, ...), custom_call_target="tpu_custom_call" | custom-call | tf_op jit(solution)/shard_map/layer/pallas_call | solution.py:317
  125.1 0.0 copy-start
  125.1 3.1 %copy.13 = f32[8,2,256,128]{3,2,1,0:T(8,128)} copy(f32[8,2,256,128]{3,2,1,0:T(8,128)} %get-tuple-element.4) | data formatting | bytes 4194304
  128.2 0.0 copy-done
  128.2 0.6 copy.14
Async XLA Ops:
  125.1 3.1 %copy-start = (f32[8,2,256]{2,1,0:T(2,128)S(1)}, f32[8,2,256]{2,1,0:T(2,128)}, u32[]{:S(2)}) copy-start(f32[8,2,256]{2,1,0:T(2,128)} %get-tuple-element.5) | copy-start | bytes 49156

commit v2 on v1

v2 whole, which is shorter than its diff:
```python
import math

import jax
import jax.numpy as jnp
import numpy as np
from jax import lax
from jax.experimental import pallas as pl
from jax.experimental.pallas import tpu as pltpu
from jax.sharding import PartitionSpec as P

MESH = pl.DeviceIdType.MESH
ROPE_BASE = 1000000.0
EPSILON = 1e-06
MASKED = 1e30
LEAST = -1e28
BF16 = jnp.bfloat16
F32 = jnp.float32

MODEL = 5120
HEAD = 128
HEADS = 8
BLOCK = 256
SPANS = 64
ROWS = 160
HALF = 80
SPLIT = 64
PART = 256
PARTS = 5
DEPTH = 8 * ROWS


def rope_tables():
    frequency = ROPE_BASE ** (-(np.arange(HEAD // 2, dtype=np.float64) * 2.0 / HEAD))
    frequency = np.concatenate([frequency, frequency])

    def table(positions):
        angles = positions[:, None].astype(np.float64) * frequency[None, :]
        return np.stack([np.cos(angles), np.sin(angles)]).astype(np.float32)

    return table(np.arange(SPANS) * BLOCK), table(np.arange(BLOCK))


def kernel(
    span_pos, tokens, w_query, w_key, w_value, query_gain, key_gain, span_table, row_table,
    out, log_sum,
    X, W, kv, q, cosine, sine, masking, summing, causal, partial, peaks, staged,
    local_sem, send_sem, recv_sem, out_sem,
):
    blk, head = lax.axis_index("blk"), lax.axis_index("head")
    z, y, c = blk // 8, (blk // 2) % 4, blk % 2
    x, l = head // 2, head % 2
    chip = blk // 2

    def place(z=z, y=y, c=c, x=x, l=l):
        return (z * 8 + y * 2 + c, x * 2 + l)

    zp, zm = place(z=(z + 1) % 4), place(z=(z + 3) % 4)
    yp, ym = place(y=(y + 1) % 4), place(y=(y + 3) % 4)
    xp, xm = place(x=(x + 1) % 4), place(x=(x + 3) % 4)
    lp, sib = place(l=1 - l), place(c=1 - c)
    nxt = (((chip + 1) % 16) * 2 + c, head)
    prv = (((chip + 15) % 16) * 2 + c, head)
    after = (((chip + 2) % 16) * 2, head)
    before = (((chip + 14) % 16) * 2 + 1, head)
    third = jnp.where(c == 0, sib[0], after[0])

    own = [pltpu.make_async_copy(w_key, W.at[0, 0, y, c, :, pl.ds(0, HEAD)], local_sem.at[0]),
           pltpu.make_async_copy(w_value, W.at[0, 0, y, c, :, pl.ds(HEAD, HEAD)], local_sem.at[1])]
    for p in range(1, PARTS):
        own.append(pltpu.make_async_copy(
            w_query.at[:, pl.ds((p - 1) * PART, PART)], W.at[p, 0, y, c], local_sem.at[1 + p]))
    own.append(pltpu.make_async_copy(tokens, X.at[:, x, l], local_sem.at[PARTS + 1]))
    for copy in own:
        copy.start()

    barrier = pltpu.get_barrier_semaphore()
    for device in (zp, zm, yp, ym, xp, xm, lp, sib, prv):
        pl.semaphore_signal(barrier, inc=1, device_id=device, device_id_type=MESH)

    @pl.when(c == 0)
    def _():
        pl.semaphore_signal(barrier, inc=1, device_id=before, device_id_type=MESH)

    pl.semaphore_wait(barrier, 9 + c)
    for copy in own:
        copy.wait()

    started = []

    def send(src, dst, device):
        n = len(started)
        copy = pltpu.make_async_remote_copy(
            src_ref=src, dst_ref=dst, send_sem=send_sem.at[n], recv_sem=recv_sem.at[n],
            device_id=device, device_id_type=MESH)
        copy.start()
        started.append(copy)
        return copy

    A, B = pl.ds(0, HALF), pl.ds(HALF, HALF)
    low, high = pl.ds(0, SPLIT), pl.ds(SPLIT, ROWS - SPLIT)
    y_below, y_above = (y + 3) % 4, (y + 1) % 4
    x_below, x_above = (x + 3) % 4, (x + 1) % 4
    all_rows, all_cols = pl.ds(0, ROWS), pl.ds(0, PART)
    left, right = pl.ds(0, HEAD), pl.ds(HEAD, HEAD)
    every_y, early, near, far, parts = pl.ds(0, 4), pl.ds(0, 3), pl.ds(1, 2), 3, pl.ds(0, PARTS)

    def z_up(p, places=y, cols=all_cols):
        return send(W.at[p, 0, places, c, all_rows, cols], W.at[p, 1, places, c, all_rows, cols], zp)

    def z_down(p, places=y, cols=all_cols):
        return send(W.at[p, 0, places, c, all_rows, cols], W.at[p, 2, places, c, all_rows, cols], zm)

    def z_on_up(p, places=y, cols=all_cols):
        return send(W.at[p, 1, places, c, A, cols], W.at[p, 3, places, c, A, cols], zp)

    def z_on_down(p, places=y, cols=all_cols):
        return send(W.at[p, 2, places, c, B, cols], W.at[p, 3, places, c, B, cols], zm)

    def y_send(device, p, slots, cols=all_cols):
        block = W.at[p, slots, y, c, all_rows, cols]
        return send(block, block, device)

    def y_on_up(p, slots, cols=all_cols):
        block = W.at[p, slots, y_below, c, low, cols]
        return send(block, block, yp)

    def y_on_down(p, slots, cols=all_cols):
        block = W.at[p, slots, y_above, c, high, cols]
        return send(block, block, ym)

    def x_send(lane, span, device):
        block = X.at[span, x, lane]
        return send(block, block, device)

    def x_on_up(lane):
        block = X.at[0, x_below, lane]
        return send(block, block, xp)

    def x_on_down(lane):
        block = X.at[1, x_above, lane]
        return send(block, block, xm)

    def core_send(p, slots=pl.ds(0, 4), cols=all_cols):
        block = W.at[p, slots, :, c, :, cols]
        return send(block, block, sib)

    def arrive(*copies):
        for copy in copies:
            copy.wait_recv()

    def tables():
        for s in range(2):
            chosen = lax.broadcasted_iota(jnp.int32, (SPANS, HEAD), 0) == span_pos[blk * 2 + s]
            span_cos = jnp.sum(jnp.where(chosen, span_table[0], 0.0), axis=0, keepdims=True)
            span_sin = jnp.sum(jnp.where(chosen, span_table[1], 0.0), axis=0, keepdims=True)
            cosine[s] = (span_cos * row_table[0] - span_sin * row_table[1]).reshape(4, 2, 32, HEAD)
            whole = span_sin * row_table[0] + span_cos * row_table[1]
            lane = lax.broadcasted_iota(jnp.int32, (BLOCK, HEAD), 1)
            sine[s] = jnp.where(lane < HEAD // 2, -whole, whole).reshape(4, 2, 32, HEAD)
        lane = lax.broadcasted_iota(jnp.int32, (HEADS, 2, 4, 2, 32, HEAD), 5)
        span = lax.broadcasted_iota(jnp.int32, (HEADS, 2, 4, 2, 32, HEAD), 1)
        q[:, :, :, :, :, pl.ds(HEAD, HEAD)] = jnp.where(lane == span, 1.0, 0.0).astype(BF16)
        for part in range(2):
            summing[part, :, pl.ds(HEAD, HEAD)] = jnp.ones((4 * BLOCK, HEAD), BF16)

    def project(p, lane):
        total = None
        for slot, place_z in enumerate((z, (z + 3) % 4, (z + 1) % 4, (z + 2) % 4)):
            depth = pl.ds(pl.multiple_of(place_z * DEPTH, DEPTH), DEPTH)
            rows = X[:, :, pl.ds(lane, 1), :, depth].reshape(BLOCK, DEPTH)
            term = jnp.dot(rows, W[p, slot].reshape(DEPTH, PART), preferred_element_type=F32)
            total = term if total is None else total + term
        return total

    def norm_rotate(raw, gain, lane):
        mean_sq = jnp.mean(raw * raw, axis=-1, keepdims=True)
        normed = raw * lax.rsqrt(mean_sq + EPSILON) * gain
        cos_rows = cosine[:, :, pl.ds(lane, 1)].reshape(BLOCK, HEAD)
        sin_rows = sine[:, :, pl.ds(lane, 1)].reshape(BLOCK, HEAD)
        turned = normed * cos_rows + pltpu.roll(normed, HEAD // 2, 1) * sin_rows
        return turned.astype(BF16).reshape(2, 4, 1, 32, HEAD)

    def keys_values(lane):
        raw = project(0, lane)
        kv[0, :, :, pl.ds(lane, 1), :, pl.ds(0, HEAD)] = norm_rotate(raw[:, :HEAD], key_gain[...], lane)
        kv[0, :, :, pl.ds(lane, 1), :, pl.ds(HEAD, HEAD)] = (
            raw[:, HEAD:].astype(BF16).reshape(2, 4, 1, 32, HEAD))

    def queries(p, lane):
        raw = project(p, lane)
        for j in range(2):
            q[2 * (p - 1) + j, :, :, pl.ds(lane, 1), :, pl.ds(0, HEAD)] = norm_rotate(
                raw[:, j * HEAD:(j + 1) * HEAD], query_gain[...], lane)

    def kv_ahead(lane):
        return send(kv.at[0, :, :, lane], kv.at[2, :, :, lane], nxt)

    def kv_third(lane):
        slot = jnp.where(c == 0, 1, 3)
        return send(kv.at[0, :, :, lane], kv.at[slot, :, :, lane], (third, head))

    def kv_across(lane):
        slot = jnp.where(c == 0, 3, 1)
        return send(kv.at[2, :, :, lane], kv.at[slot, :, :, lane], sib)

    own_pos = [span_pos[blk * 2 + s] for s in range(2)]

    def gather_keys(lane, part):
        column = lax.broadcasted_iota(jnp.int32, (HEAD, HEAD), 1)
        for step in range(4):
            source = (blk + 32 - step) % 32
            block = kv[step, :, :, pl.ds(lane, 1)].reshape(BLOCK, 2 * HEAD)
            rows = pl.ds(step * BLOCK, BLOCK)
            masking[part, rows, pl.ds(0, HEAD)] = block[:, :HEAD]
            summing[part, rows, pl.ds(0, HEAD)] = block[:, HEAD:]
            for s in range(2):
                pos = span_pos[source * 2 + s]
                hide = [jnp.where(pos <= own_pos[i], 0.0, -MASKED).astype(F32) for i in range(2)]
                masking[part, pl.ds(step * BLOCK + s * HEAD, HEAD), pl.ds(HEAD, HEAD)] = jnp.where(
                    column == 0, hide[0], jnp.where(column == 1, hide[1], 0.0)).astype(BF16)
        key = lax.broadcasted_iota(jnp.int32, (BLOCK, HEAD), 1)
        place_in = key // 32 * 64 + lane * 32 + key % 32
        hidden = jnp.where(lax.broadcasted_iota(jnp.int32, (BLOCK, HEAD), 0) >= place_in, 0.0, -MASKED)
        for i in range(2):
            causal[part, pl.ds(i * BLOCK, BLOCK), pl.ds(i * HEAD, HEAD)] = hidden
            causal[part, pl.ds(i * BLOCK, BLOCK), pl.ds((1 - i) * HEAD, HEAD)] = jnp.zeros((BLOCK, HEAD), F32)

    factor = HEAD ** (-0.5) * math.log2(math.e)

    def attend(p, half):
        first = half == 0
        for h in (2 * p - 2, 2 * p - 1):
            rows = q[h].reshape(2 * BLOCK, 2 * HEAD)
            peak = None
            found = []
            for step in range(4):
                keys = masking[half, pl.ds(step * BLOCK, BLOCK), :]
                part = lax.dot_general(rows, keys, (((1,), (1,)), ((), ())), preferred_element_type=F32) * factor
                if step == 0:
                    part = part + causal[half]
                found.append(part)
                top = jnp.maximum(part[:, :HEAD], part[:, HEAD:])
                peak = top if peak is None else jnp.maximum(peak, top)
            peak = jnp.max(peak, axis=-1, keepdims=True)
            if first:
                peak = jnp.maximum(peak, LEAST)
            else:
                before_peak = peaks[h][:, 0:1]
                peak = jnp.maximum(peak, before_peak)
            weights = jnp.concatenate([jnp.exp2(part - peak).astype(BF16) for part in found], axis=1)
            summed = jnp.dot(weights, summing[half], preferred_element_type=F32)
            if first:
                partial[h] = summed
                peaks[h] = jnp.broadcast_to(peak, (2 * BLOCK, HEAD))
            else:
                summed = summed + partial[h] * jnp.exp2(before_peak - peak)
                whole = summed[:, HEAD:]
                staged[h] = (summed[:, :HEAD] / whole).reshape(2, BLOCK, HEAD)
                lse = jnp.transpose(peak * math.log(2.0) + jnp.log(whole))
                for i in range(2):
                    log_sum[h, pl.ds(i, 1), :] = lse[0:1, i * BLOCK:(i + 1) * BLOCK]
                pltpu.make_async_copy(staged.at[h], out.at[h], out_sem.at[h]).start()

    z0_p = z_up(0)
    ya_m = y_send(ym, parts, 0)
    z0_m = z_down(0)
    z1_m = z_down(1)
    z1_p = z_up(1)
    lane_b = x_send(l, 1, lp)
    xo_a_p = x_send(l, 0, xp)
    xo_b_m = x_send(l, 1, xm)
    ya_p = y_send(yp, parts, 0)
    arrive(z0_p)
    z0_fp = z_on_up(0)
    arrive(z0_m)
    y0_m = y_send(ym, 0, near)
    xo_a_m = x_send(l, 0, xm)
    xo_b_p = x_send(l, 1, xp)
    z0_fm = z_on_down(0)
    arrive(z1_p, z1_m)
    y1_m = y_send(ym, 1, near)
    y0_p = y_send(yp, 0, near)
    arrive(ya_m)
    ya_fm = y_on_down(parts, 0)
    z1_fp = z_on_up(1)
    arrive(ya_p)
    ya_fp = y_on_up(parts, 0)
    tables()
    arrive(y0_m)
    y0_fm = y_on_down(0, near)
    z2_m = z_down(2)
    z2_p = z_up(2)
    arrive(lane_b)
    xt_b_p = x_send(1 - l, 1, xp)
    z1_fm = z_on_down(1)
    arrive(xo_a_p)
    xo_fa = x_on_up(l)
    lane_a = x_send(l, 0, lp)
    y1_p = y_send(yp, 1, near)
    arrive(y0_p)
    y0_fp = y_on_up(0, near)
    arrive(y1_m)
    y1_fm = y_on_down(1, near)
    xt_b_m = x_send(1 - l, 1, xm)
    arrive(z0_fp, z0_fm)
    y0s_p = y_send(yp, 0, far)
    arrive(y1_p)
    y1_fp = y_on_up(1, near)
    arrive(z1_fp, z1_fm)
    y1s_p = y_send(yp, 1, far)
    y0s_m = y_send(ym, 0, far)
    y1s_m = y_send(ym, 1, far)
    arrive(z2_m)
    z2_fm = z_on_down(2)
    arrive(z2_p)
    z2_fp = z_on_up(2)
    y2_m = y_send(ym, 2, near)
    arrive(xo_b_m)
    xo_fb = x_on_down(l)
    arrive(y0_fp, y0_fm, ya_fp, ya_fm)
    c0n = core_send(0, early)
    arrive(y0s_p)
    y0s_fp = y_on_up(0, far)
    y2_p = y_send(yp, 2, near)
    arrive(y1_fp, y1_fm)
    c1n = core_send(1, early)
    z3_p = z_up(3)
    arrive(y0s_m)
    y0s_fm = y_on_down(0, far)
    z3_m = z_down(3)
    arrive(lane_a)
    xt_a_p = x_send(1 - l, 0, xp)
    zL_p = z_up(4, cols=left)
    xt_a_m = x_send(1 - l, 0, xm)
    arrive(y1s_p)
    y1s_fp = y_on_up(1, far)
    zL_m = z_down(4, cols=left)
    arrive(y1s_m)
    y1s_fm = y_on_down(1, far)
    arrive(z2_fp, z2_fm)
    y2s_p = y_send(yp, 2, far)
    arrive(y2_m)
    y2_fm = y_on_down(2, near)
    y2s_m = y_send(ym, 2, far)
    arrive(y2_p)
    y2_fp = y_on_up(2, near)
    zR_p = z_up(4, every_y, right)
    zR_m = z_down(4, every_y, right)
    arrive(y0s_fp, y0s_fm)
    c0f = core_send(0, far)
    arrive(z3_p, z3_m)
    y3_p = y_send(yp, 3, near)
    arrive(y1s_fp, y1s_fm)
    c1f = core_send(1, far)
    arrive(xt_b_m)
    xt_fb = x_on_down(1 - l)
    y3_m = y_send(ym, 3, near)
    z3_fp = z_on_up(3)
    arrive(zL_p, zL_m)
    yL_m = y_send(ym, 4, near, cols=left)
    arrive(c0n, c0f, xo_b_p, xo_a_m, xo_fa, xo_fb)
    keys_values(l)
    arrive(xt_a_p)
    xt_fa = x_on_up(1 - l)
    knA = kv_ahead(l)
    yL_p = y_send(yp, 4, near, cols=left)
    z3_fm = z_on_down(3)
    arrive(y2s_m)
    y2s_fm = y_on_down(2, far)
    arrive(y2s_p)
    y2s_fp = y_on_up(2, far)
    zL_fm = z_on_down(4, cols=left)
    zL_fp = z_on_up(4, cols=left)
    arrive(y3_p)
    y3_fp = y_on_up(3, near)
    arrive(y2_fp, y2_fm)
    c2n = core_send(2, early)
    arrive(y3_m)
    y3_fm = y_on_down(3, near)
    arrive(zR_p)
    zR_fp = z_on_up(4, every_y, right)
    arrive(zR_m)
    zR_fm = z_on_down(4, every_y, right)
    arrive(c1n, c1f)
    queries(1, l)
    k3A = kv_third(l)
    arrive(z3_fp, z3_fm)
    y3s_p = y_send(yp, 3, far)
    y3s_m = y_send(ym, 3, far)
    arrive(knA)
    kfA = kv_across(l)
    arrive(yL_p)
    yL_fp = y_on_up(4, near, cols=left)
    arrive(yL_m)
    yL_fm = y_on_down(4, near, cols=left)
    arrive(y2s_fp, y2s_fm)
    c2f = core_send(2, far)
    arrive(zL_fp, zL_fm)
    yLs_p = y_send(yp, 4, far, cols=left)
    yLs_m = y_send(ym, 4, far, cols=left)
    arrive(xt_b_p, xt_a_m, xt_fa, xt_fb)
    keys_values(1 - l)
    k3B = kv_third(1 - l)
    knB = kv_ahead(1 - l)
    queries(1, 1 - l)
    arrive(k3A, kfA)
    gather_keys(l, 0)
    attend(1, 0)
    arrive(y3_fp, y3_fm)
    c3n = core_send(3, early)
    arrive(y3s_m)
    y3s_fm = y_on_down(3, far)
    arrive(y3s_p)
    y3s_fp = y_on_up(3, far)
    arrive(zR_fp, zR_fm)
    c4b = core_send(4, cols=right)
    arrive(yLs_p)
    yLs_fp = y_on_up(4, far, cols=left)
    arrive(c2n, c2f)
    queries(2, 1 - l)
    arrive(yLs_m)
    yLs_fm = y_on_down(4, far, cols=left)
    queries(2, l)
    arrive(knB)
    kfB = kv_across(1 - l)
    attend(2, 0)
    arrive(y3s_fp, y3s_fm)
    c3f = core_send(3, far)
    arrive(yL_fp, yL_fm, yLs_fp, yLs_fm)
    c4a = core_send(4, cols=left)
    arrive(k3B, kfB)
    gather_keys(1 - l, 1)
    attend(2, 1)
    attend(1, 1)
    arrive(c3n, c3f)
    queries(3, 1 - l)
    queries(3, l)
    arrive(c4a, c4b)
    queries(4, 1 - l)
    attend(3, 0)
    queries(4, l)
    attend(3, 1)
    attend(4, 0)
    attend(4, 1)

    def finish(h, carry):
        pltpu.make_async_copy(staged.at[h], out.at[h], out_sem.at[h]).wait()
        return carry

    lax.fori_loop(0, HEADS, finish, 0)
    for copy in started:
        copy.wait_send()


SENDS = 98


def shards(tokens, span_pos, w_query, key_projection, value_projection, query_gain, key_gain):
    span_table, row_table = rope_tables()
    vmem, anywhere = pl.BlockSpec(memory_space=pltpu.VMEM), pl.BlockSpec(memory_space=pl.ANY)
    hbm = pl.BlockSpec(memory_space=pltpu.HBM)
    return pl.pallas_call(
        kernel,
        out_shape=(
            jax.ShapeDtypeStruct((HEADS, 2, BLOCK, HEAD), F32),
            jax.ShapeDtypeStruct((HEADS, 2, BLOCK), F32),
        ),
        in_specs=[pl.BlockSpec(memory_space=pltpu.SMEM), hbm, hbm, hbm, hbm, vmem, vmem, vmem, vmem],
        out_specs=(anywhere, vmem),
        scratch_shapes=[
            pltpu.VMEM((2, 4, 2, 32, MODEL), BF16),
            pltpu.VMEM((PARTS, 4, 4, 2, ROWS, PART), BF16),
            pltpu.VMEM((4, 2, 4, 2, 32, 2 * HEAD), BF16),
            pltpu.VMEM((HEADS, 2, 4, 2, 32, 2 * HEAD), BF16),
            pltpu.VMEM((2, 4, 2, 32, HEAD), F32),
            pltpu.VMEM((2, 4, 2, 32, HEAD), F32),
            pltpu.VMEM((2, 4 * BLOCK, 2 * HEAD), BF16),
            pltpu.VMEM((2, 4 * BLOCK, 2 * HEAD), BF16),
            pltpu.VMEM((2, 2 * BLOCK, 2 * HEAD), F32),
            pltpu.VMEM((HEADS, 2 * BLOCK, 2 * HEAD), F32),
            pltpu.VMEM((HEADS, 2 * BLOCK, HEAD), F32),
            pltpu.VMEM((HEADS, 2, BLOCK, HEAD), F32),
            pltpu.SemaphoreType.DMA((PARTS + 2,)),
            pltpu.SemaphoreType.DMA((SENDS,)),
            pltpu.SemaphoreType.DMA((SENDS,)),
            pltpu.SemaphoreType.DMA((HEADS,)),
        ],
        compiler_params=pltpu.CompilerParams(
            collective_id=0, has_side_effects=True, vmem_limit_bytes=56 * 2**20),
        name="layer",
    )(span_pos, tokens, w_query, key_projection, value_projection, query_gain[None], key_gain[None],
      span_table, row_table)


def solution(mesh):
    placed = (
        P("blk", "head", None),
        P(),
        P("blk", "head"),
        P("blk", "head"),
        P("blk", "head"),
        P(),
        P(),
    )
    return jax.shard_map(
        shards,
        mesh=mesh,
        in_specs=placed,
        out_specs=(P("head", "blk", None, None), P("head", "blk", None)),
        check_vma=False,
    )
```

time: 129 us -> 103 us (0.80)
  the two profiles are of different devices: /device:TPU:2 before, /device:TPU:40 now
where the time goes in v2:
time: 103 us
  Pallas kernels  98.8 us (96%)
  local copies, waits for them, and re-layouts  3.73 us (4%)
    pallas_call x1, Pallas kernels, shards(): pl.pallas_call(kernel, out_shape=(jax.ShapeDtypeStruct((HEADS, 2, BLOCK,...  98.8 us
    unnamed x4, local copies, waits for them, and re-layouts  3.73 us

profile of v2, /device:TPU:40, one launch (start us, length us, event | category | flops | bytes accessed | tf_op | source)
XLA Modules:
  0.0 103.2 jit_solution(10419943408071639272)
XLA Ops:
  0.6 98.8 %layer.1 = (f32[8,2,256,128]{3,2,1,0:T(8,128)}, f32[8,2,256]{2,1,0:T(2,128)}) custom-call(s32[64]{0:T(128)} %span_pos.1, bf16[2,32,5120]{2,1,0:T(8,128)(2,1)} %tokens.1, bf16[160,1024]{1,0:T(8,128)(2,1)} %w_query.1, bf16[160,128]{1,0:T(8,128)(2,1)} %w_key.1, bf16[160,128]{1,0:T(8,128)(2,1)} %w_value.1, f32[1,128]{1,0:T(1,128)} %bitcast.2, f32[1,128]{1,0:T(1,128)} %bitcast.3, ...), custom_call_target="tpu_custom_call" | custom-call | tf_op jit(solution)/shard_map/layer/pallas_call | solution.py:462
  99.4 0.0 copy-start
  99.4 3.1 %copy.13 = f32[8,2,256,128]{3,2,1,0:T(8,128)} copy(f32[8,2,256,128]{3,2,1,0:T(8,128)} %get-tuple-element.4) | data formatting | bytes 4194304
  102.6 0.0 copy-done
  102.6 0.6 copy.14
Async XLA Ops:
  99.4 3.1 %copy-start = (f32[8,2,256]{2,1,0:T(2,128)S(1)}, f32[8,2,256]{2,1,0:T(2,128)}, u32[]{:S(2)}) copy-start(f32[8,2,256]{2,1,0:T(2,128)} %get-tuple-element.5) | copy-start | bytes 49156

commit v3 on v2

--- a/solution.py
+++ b/solution.py
@@ -54,7 +54,8 @@
     def place(z=z, y=y, c=c, x=x, l=l):
         return (z * 8 + y * 2 + c, x * 2 + l)
 
-    zp, zm = place(z=(z + 1) % 4), place(z=(z + 3) % 4)
+    z_up_at, z_down_at = (z + 1 + 2 * l) % 4, (z + 3 + 2 * l) % 4
+    zp, zm = place(z=z_up_at), place(z=z_down_at)
     yp, ym = place(y=(y + 1) % 4), place(y=(y + 3) % 4)
     xp, xm = place(x=(x + 1) % 4), place(x=(x + 3) % 4)
     lp, sib = place(l=1 - l), place(c=1 - c)
@@ -165,7 +166,7 @@
 
     def project(p, lane):
         total = None
-        for slot, place_z in enumerate((z, (z + 3) % 4, (z + 1) % 4, (z + 2) % 4)):
+        for slot, place_z in enumerate((z, z_down_at, z_up_at, (z + 2) % 4)):
             depth = pl.ds(pl.multiple_of(place_z * DEPTH, DEPTH), DEPTH)
             rows = X[:, :, pl.ds(lane, 1), :, depth].reshape(BLOCK, DEPTH)
             term = jnp.dot(rows, W[p, slot].reshape(DEPTH, PART), preferred_element_type=F32)
@@ -205,14 +206,10 @@
 
     own_pos = [span_pos[blk * 2 + s] for s in range(2)]
 
-    def gather_keys(lane, part):
+    def mask_keys(lane, part):
         column = lax.broadcasted_iota(jnp.int32, (HEAD, HEAD), 1)
         for step in range(4):
             source = (blk + 32 - step) % 32
-            block = kv[step, :, :, pl.ds(lane, 1)].reshape(BLOCK, 2 * HEAD)
-            rows = pl.ds(step * BLOCK, BLOCK)
-            masking[part, rows, pl.ds(0, HEAD)] = block[:, :HEAD]
-            summing[part, rows, pl.ds(0, HEAD)] = block[:, HEAD:]
             for s in range(2):
                 pos = span_pos[source * 2 + s]
                 hide = [jnp.where(pos <= own_pos[i], 0.0, -MASKED).astype(F32) for i in range(2)]
@@ -224,6 +221,13 @@
         for i in range(2):
             causal[part, pl.ds(i * BLOCK, BLOCK), pl.ds(i * HEAD, HEAD)] = hidden
             causal[part, pl.ds(i * BLOCK, BLOCK), pl.ds((1 - i) * HEAD, HEAD)] = jnp.zeros((BLOCK, HEAD), F32)
+
+    def gather_keys(lane, part):
+        for step in range(4):
+            block = kv[step, :, :, pl.ds(lane, 1)].reshape(BLOCK, 2 * HEAD)
+            rows = pl.ds(step * BLOCK, BLOCK)
+            masking[part, rows, pl.ds(0, HEAD)] = block[:, :HEAD]
+            summing[part, rows, pl.ds(0, HEAD)] = block[:, HEAD:]
 
     factor = HEAD ** (-0.5) * math.log2(math.e)
 
@@ -261,186 +265,189 @@
                     log_sum[h, pl.ds(i, 1), :] = lse[0:1, i * BLOCK:(i + 1) * BLOCK]
                 pltpu.make_async_copy(staged.at[h], out.at[h], out_sem.at[h]).start()
 
-    z0_p = z_up(0)
+    z2_p = z_up(2)
+    z2_m = z_down(2)
     ya_m = y_send(ym, parts, 0)
     z0_m = z_down(0)
+    z0_p = z_up(0)
+    lane_b = x_send(l, 1, lp)
     z1_m = z_down(1)
-    z1_p = z_up(1)
-    lane_b = x_send(l, 1, lp)
     xo_a_p = x_send(l, 0, xp)
+    ya_p = y_send(yp, parts, 0)
     xo_b_m = x_send(l, 1, xm)
-    ya_p = y_send(yp, parts, 0)
-    arrive(z0_p)
-    z0_fp = z_on_up(0)
-    arrive(z0_m)
-    y0_m = y_send(ym, 0, near)
-    xo_a_m = x_send(l, 0, xm)
-    xo_b_p = x_send(l, 1, xp)
-    z0_fm = z_on_down(0)
-    arrive(z1_p, z1_m)
-    y1_m = y_send(ym, 1, near)
-    y0_p = y_send(yp, 0, near)
-    arrive(ya_m)
-    ya_fm = y_on_down(parts, 0)
-    z1_fp = z_on_up(1)
-    arrive(ya_p)
-    ya_fp = y_on_up(parts, 0)
-    tables()
-    arrive(y0_m)
-    y0_fm = y_on_down(0, near)
-    z2_m = z_down(2)
-    z2_p = z_up(2)
-    arrive(lane_b)
-    xt_b_p = x_send(1 - l, 1, xp)
-    z1_fm = z_on_down(1)
-    arrive(xo_a_p)
-    xo_fa = x_on_up(l)
-    lane_a = x_send(l, 0, lp)
-    y1_p = y_send(yp, 1, near)
-    arrive(y0_p)
-    y0_fp = y_on_up(0, near)
-    arrive(y1_m)
-    y1_fm = y_on_down(1, near)
-    xt_b_m = x_send(1 - l, 1, xm)
-    arrive(z0_fp, z0_fm)
-    y0s_p = y_send(yp, 0, far)
-    arrive(y1_p)
-    y1_fp = y_on_up(1, near)
-    arrive(z1_fp, z1_fm)
-    y1s_p = y_send(yp, 1, far)
-    y0s_m = y_send(ym, 0, far)
-    y1s_m = y_send(ym, 1, far)
     arrive(z2_m)
     z2_fm = z_on_down(2)
     arrive(z2_p)
+    y2_p = y_send(yp, 2, near)
+    tables()
+    mask_keys(l, 0)
+    mask_keys(1 - l, 1)
     z2_fp = z_on_up(2)
+    xo_a_m = x_send(l, 0, xm)
+    z1_p = z_up(1)
     y2_m = y_send(ym, 2, near)
+    xo_b_p = x_send(l, 1, xp)
+    arrive(z0_p, z0_m)
+    y0_m = y_send(ym, 0, near)
+    z0_fp = z_on_up(0)
+    z0_fm = z_on_down(0)
     arrive(xo_b_m)
     xo_fb = x_on_down(l)
-    arrive(y0_fp, y0_fm, ya_fp, ya_fm)
-    c0n = core_send(0, early)
-    arrive(y0s_p)
-    y0s_fp = y_on_up(0, far)
-    y2_p = y_send(yp, 2, near)
-    arrive(y1_fp, y1_fm)
-    c1n = core_send(1, early)
+    arrive(ya_m)
+    ya_fm = y_on_down(parts, 0)
+    y0_p = y_send(yp, 0, near)
+    arrive(y2_m)
+    y2_fm = y_on_down(2, near)
+    arrive(xo_a_p)
+    xo_fa = x_on_up(l)
+    arrive(y2_p)
+    y2_fp = y_on_up(2, near)
+    arrive(ya_p)
+    ya_fp = y_on_up(parts, 0)
+    arrive(lane_b)
+    xt_b_p = x_send(1 - l, 1, xp)
+    arrive(y0_p)
+    y0_fp = y_on_up(0, near)
+    lane_a = x_send(l, 0, lp)
+    arrive(z1_m)
+    z1_fm = z_on_down(1)
+    arrive(y0_m)
+    y0_fm = y_on_down(0, near)
+    arrive(z1_p)
+    z1_fp = z_on_up(1)
+    arrive(z2_fp, z2_fm)
+    y2s_m = y_send(ym, 2, far)
+    y2s_p = y_send(yp, 2, far)
+    arrive(z0_fp, z0_fm)
+    y0s_p = y_send(yp, 0, far)
     z3_p = z_up(3)
-    arrive(y0s_m)
-    y0s_fm = y_on_down(0, far)
     z3_m = z_down(3)
+    y0s_m = y_send(ym, 0, far)
+    y1_m = y_send(ym, 1, near)
+    xt_b_m = x_send(1 - l, 1, xm)
+    y1_p = y_send(yp, 1, near)
+    zL_m = z_down(4, cols=left)
     arrive(lane_a)
     xt_a_p = x_send(1 - l, 0, xp)
     zL_p = z_up(4, cols=left)
+    arrive(y2s_p)
+    y2s_fp = y_on_up(2, far)
     xt_a_m = x_send(1 - l, 0, xm)
+    arrive(y0s_p)
+    y0s_fp = y_on_up(0, far)
+    arrive(y2s_m)
+    y2s_fm = y_on_down(2, far)
+    arrive(y2_fp, y2_fm, ya_fp, ya_fm)
+    c2n = core_send(2, early)
+    arrive(y0_fp, y0_fm)
+    c0n = core_send(0, early)
+    arrive(y0s_m)
+    y0s_fm = y_on_down(0, far)
+    zR_m = z_down(4, every_y, right)
+    arrive(z1_fp, z1_fm)
+    y1s_m = y_send(ym, 1, far)
+    zR_p = z_up(4, every_y, right)
+    y1s_p = y_send(yp, 1, far)
+    arrive(y1_m)
+    y1_fm = y_on_down(1, near)
+    arrive(y1_p)
+    y1_fp = y_on_up(1, near)
+    arrive(y2s_fp, y2s_fm)
+    c2f = core_send(2, far)
+    arrive(z3_p, z3_m)
+    y3_p = y_send(yp, 3, near)
+    y3_m = y_send(ym, 3, near)
+    arrive(y0s_fp, y0s_fm)
+    c0f = core_send(0, far)
+    arrive(y1s_m)
+    y1s_fm = y_on_down(1, far)
     arrive(y1s_p)
     y1s_fp = y_on_up(1, far)
-    zL_m = z_down(4, cols=left)
-    arrive(y1s_m)
-    y1s_fm = y_on_down(1, far)
-    arrive(z2_fp, z2_fm)
-    y2s_p = y_send(yp, 2, far)
-    arrive(y2_m)
-    y2_fm = y_on_down(2, near)
-    y2s_m = y_send(ym, 2, far)
-    arrive(y2_p)
-    y2_fp = y_on_up(2, near)
-    zR_p = z_up(4, every_y, right)
-    zR_m = z_down(4, every_y, right)
-    arrive(y0s_fp, y0s_fm)
-    c0f = core_send(0, far)
-    arrive(z3_p, z3_m)
-    y3_p = y_send(yp, 3, near)
-    arrive(y1s_fp, y1s_fm)
-    c1f = core_send(1, far)
     arrive(xt_b_m)
     xt_fb = x_on_down(1 - l)
-    y3_m = y_send(ym, 3, near)
-    z3_fp = z_on_up(3)
-    arrive(zL_p, zL_m)
+    arrive(zL_m)
+    zL_fm = z_on_down(4, cols=left)
+    arrive(zL_p)
+    yL_p = y_send(yp, 4, near, cols=left)
+    arrive(xt_a_p)
+    xt_fa = x_on_up(1 - l)
+    z3_fm = z_on_down(3)
+    zL_fp = z_on_up(4, cols=left)
     yL_m = y_send(ym, 4, near, cols=left)
+    arrive(y1_fp, y1_fm)
+    c1n = core_send(1, early)
     arrive(c0n, c0f, xo_b_p, xo_a_m, xo_fa, xo_fb)
     keys_values(l)
-    arrive(xt_a_p)
-    xt_fa = x_on_up(1 - l)
-    knA = kv_ahead(l)
-    yL_p = y_send(yp, 4, near, cols=left)
-    z3_fm = z_on_down(3)
-    arrive(y2s_m)
-    y2s_fm = y_on_down(2, far)
-    arrive(y2s_p)
-    y2s_fp = y_on_up(2, far)
-    zL_fm = z_on_down(4, cols=left)
-    zL_fp = z_on_up(4, cols=left)
+    z3_fp = z_on_up(3)
     arrive(y3_p)
     y3_fp = y_on_up(3, near)
-    arrive(y2_fp, y2_fm)
-    c2n = core_send(2, early)
+    knA = kv_ahead(l)
     arrive(y3_m)
     y3_fm = y_on_down(3, near)
     arrive(zR_p)
     zR_fp = z_on_up(4, every_y, right)
+    arrive(y1s_fp, y1s_fm)
+    c1f = core_send(1, far)
+    k3A = kv_third(l)
+    arrive(zL_fp, zL_fm)
+    yLs_p = y_send(yp, 4, far, cols=left)
     arrive(zR_m)
     zR_fm = z_on_down(4, every_y, right)
+    arrive(c2n, c2f)
+    queries(2, l)
+    arrive(yL_p)
+    yL_fp = y_on_up(4, near, cols=left)
+    arrive(z3_fp, z3_fm)
+    y3s_m = y_send(ym, 3, far)
+    yLs_m = y_send(ym, 4, far, cols=left)
+    y3s_p = y_send(yp, 3, far)
     arrive(c1n, c1f)
     queries(1, l)
-    k3A = kv_third(l)
-    arrive(z3_fp, z3_fm)
-    y3s_p = y_send(yp, 3, far)
-    y3s_m = y_send(ym, 3, far)
-    arrive(knA)
-    kfA = kv_across(l)
-    arrive(yL_p)
-    yL_fp = y_on_up(4, near, cols=left)
-    arrive(yL_m)
-    yL_fm = y_on_down(4, near, cols=left)
-    arrive(y2s_fp, y2s_fm)
-    c2f = core_send(2, far)
-    arrive(zL_fp, zL_fm)
-    yLs_p = y_send(yp, 4, far, cols=left)
-    yLs_m = y_send(ym, 4, far, cols=left)
     arrive(xt_b_p, xt_a_m, xt_fa, xt_fb)
     keys_values(1 - l)
+    knB = kv_ahead(1 - l)
     k3B = kv_third(1 - l)
-    knB = kv_ahead(1 - l)
-    queries(1, 1 - l)
-    arrive(k3A, kfA)
-    gather_keys(l, 0)
-    attend(1, 0)
+    queries(2, 1 - l)
     arrive(y3_fp, y3_fm)
     c3n = core_send(3, early)
+    queries(1, 1 - l)
+    arrive(yLs_p)
+    yLs_fp = y_on_up(4, far, cols=left)
     arrive(y3s_m)
     y3s_fm = y_on_down(3, far)
     arrive(y3s_p)
     y3s_fp = y_on_up(3, far)
     arrive(zR_fp, zR_fm)
     c4b = core_send(4, cols=right)
-    arrive(yLs_p)
-    yLs_fp = y_on_up(4, far, cols=left)
-    arrive(c2n, c2f)
-    queries(2, 1 - l)
+    arrive(yL_m)
+    yL_fm = y_on_down(4, near, cols=left)
     arrive(yLs_m)
     yLs_fm = y_on_down(4, far, cols=left)
-    queries(2, l)
-    arrive(knB)
-    kfB = kv_across(1 - l)
+    arrive(knA)
+    kfA = kv_across(l)
+    arrive(k3A, kfA)
+    gather_keys(l, 0)
     attend(2, 0)
+    attend(1, 0)
     arrive(y3s_fp, y3s_fm)
     c3f = core_send(3, far)
     arrive(yL_fp, yL_fm, yLs_fp, yLs_fm)
     c4a = core_send(4, cols=left)
+    arrive(c3n, c3f)
+    queries(3, l)
+    queries(3, 1 - l)
+    arrive(knB)
+    kfB = kv_across(1 - l)
+    attend(3, 0)
+    arrive(c4a, c4b)
+    queries(4, l)
+    queries(4, 1 - l)
+    attend(4, 0)
     arrive(k3B, kfB)
     gather_keys(1 - l, 1)
     attend(2, 1)
     attend(1, 1)
-    arrive(c3n, c3f)
-    queries(3, 1 - l)
-    queries(3, l)
-    arrive(c4a, c4b)
-    queries(4, 1 - l)
-    attend(3, 0)
-    queries(4, l)
     attend(3, 1)
-    attend(4, 0)
     attend(4, 1)
 
     def finish(h, carry):

time: 103 us -> 101 us (0.981)
  the two profiles are of different devices: /device:TPU:40 before, /device:TPU:2 now
where the time goes in v3:
time: 101 us; the launch traced here: 100 us
  Pallas kernels  96.1 us (95%)
  local copies, waits for them, and re-layouts  3.73 us (4%)
    pallas_call x1, Pallas kernels, shards(): pl.pallas_call(kernel, out_shape=(jax.ShapeDtypeStruct((HEADS, 2, BLOCK,...  96.1 us
    unnamed x4, local copies, waits for them, and re-layouts  3.73 us

profile of v3, /device:TPU:2, one launch (start us, length us, event | category | flops | bytes accessed | tf_op | source)
XLA Modules:
  0.0 100.5 jit_solution(6408460480410460164)
XLA Ops:
  0.6 96.1 %layer.1 = (f32[8,2,256,128]{3,2,1,0:T(8,128)}, f32[8,2,256]{2,1,0:T(2,128)}) custom-call(s32[64]{0:T(128)} %span_pos.1, bf16[2,32,5120]{2,1,0:T(8,128)(2,1)} %tokens.1, bf16[160,1024]{1,0:T(8,128)(2,1)} %w_query.1, bf16[160,128]{1,0:T(8,128)(2,1)} %w_key.1, bf16[160,128]{1,0:T(8,128)(2,1)} %w_value.1, f32[1,128]{1,0:T(1,128)} %bitcast.2, f32[1,128]{1,0:T(1,128)} %bitcast.3, ...), custom_call_target="tpu_custom_call" | custom-call | tf_op jit(solution)/shard_map/layer/pallas_call | solution.py:469
  96.7 0.0 copy-start
  96.7 3.1 %copy.13 = f32[8,2,256,128]{3,2,1,0:T(8,128)} copy(f32[8,2,256,128]{3,2,1,0:T(8,128)} %get-tuple-element.4) | data formatting | bytes 4194304
  99.9 0.0 copy-done
  99.9 0.6 copy.14
Async XLA Ops:
  96.7 3.1 %copy-start = (f32[8,2,256]{2,1,0:T(2,128)S(1)}, f32[8,2,256]{2,1,0:T(2,128)}, u32[]{:S(2)}) copy-start(f32[8,2,256]{2,1,0:T(2,128)} %get-tuple-element.5) | copy-start | bytes 49156

commit v4 on v3

--- a/solution.py
+++ b/solution.py
@@ -233,6 +233,7 @@
 
     def attend(p, half):
         first = half == 0
+        pair = {}
         for h in (2 * p - 2, 2 * p - 1):
             rows = q[h].reshape(2 * BLOCK, 2 * HEAD)
             peak = None
@@ -245,7 +246,8 @@
                 found.append(part)
                 top = jnp.maximum(part[:, :HEAD], part[:, HEAD:])
                 peak = top if peak is None else jnp.maximum(peak, top)
-            peak = jnp.max(peak, axis=-1, keepdims=True)
+            pair[h] = found, jnp.max(peak, axis=-1, keepdims=True)
+        for h, (found, peak) in pair.items():
             if first:
                 peak = jnp.maximum(peak, LEAST)
             else:

time: 101 us -> 101 us (level)
  no operation moved by 1% of the time
where the time goes in v4:
time: 101 us; the launch traced here: 100 us
  Pallas kernels  96.1 us (95%)
  local copies, waits for them, and re-layouts  3.73 us (4%)
    pallas_call x1, Pallas kernels, shards(): pl.pallas_call(kernel, out_shape=(jax.ShapeDtypeStruct((HEADS, 2, BLOCK,...  96.1 us
    unnamed x4, local copies, waits for them, and re-layouts  3.73 us

profile of v4, /device:TPU:2, one launch (start us, length us, event | category | flops | bytes accessed | tf_op | source)
XLA Modules:
  0.0 100.5 jit_solution(3922456164601002148)
XLA Ops:
  0.6 96.1 %layer.1 = (f32[8,2,256,128]{3,2,1,0:T(8,128)}, f32[8,2,256]{2,1,0:T(2,128)}) custom-call(s32[64]{0:T(128)} %span_pos.1, bf16[2,32,5120]{2,1,0:T(8,128)(2,1)} %tokens.1, bf16[160,1024]{1,0:T(8,128)(2,1)} %w_query.1, bf16[160,128]{1,0:T(8,128)(2,1)} %w_key.1, bf16[160,128]{1,0:T(8,128)(2,1)} %w_value.1, f32[1,128]{1,0:T(1,128)} %bitcast.2, f32[1,128]{1,0:T(1,128)} %bitcast.3, ...), custom_call_target="tpu_custom_call" | custom-call | tf_op jit(solution)/shard_map/layer/pallas_call | solution.py:471
  96.8 0.0 copy-start
  96.8 3.1 %copy.13 = f32[8,2,256,128]{3,2,1,0:T(8,128)} copy(f32[8,2,256,128]{3,2,1,0:T(8,128)} %get-tuple-element.4) | data formatting | bytes 4194304
  99.9 0.0 copy-done
  99.9 0.6 copy.14
Async XLA Ops:
  96.8 3.1 %copy-start = (f32[8,2,256]{2,1,0:T(2,128)S(1)}, f32[8,2,256]{2,1,0:T(2,128)}, u32[]{:S(2)}) copy-start(f32[8,2,256]{2,1,0:T(2,128)} %get-tuple-element.5) | copy-start | bytes 49156
